TPU v7x, 32 devices: a whole 2x2x4 slice. The times are simulated.
32 devices in a mesh: gx: 2 (over x), gy: 4 (over y, core), gz: 4 (over z).
Axes of the slice: x: 2, y: 2, z: 4, core: 2. Of those that a mesh axis runs over, the one named last changes fastest.
Arguments:
- right_side: float32 [16, 64, 1024], P('gx', 'gy', 'gz'), may hold values from -6 to 6
- coefficient: float32 [16, 64, 1024], P('gx', 'gy', 'gz'), may hold values from 0.3 to 3
- agg_weight: float32 [16, 64, 1024], P('gx', 'gy', 'gz'), may hold values from 0.03 to 0.1
- coarse_factor: float32 [256, 256], P(('gx', 'gy', 'gz')), may hold values from -0.75 to 0.75
Outputs:
- pressure_update: float32 [16, 64, 1024], P('gx', 'gy', 'gz')
- coarse_solution: float32 [256], P(('gx', 'gy', 'gz'))
All inputs are finite; a program needn't handle non-finite values.
Results may differ from a plain program's by a relative error of at most 0.00024.
Values sent between devices are 32-bit elements; how exact they have to be, the bound alone decides.
A program may use at most 64 MiB of HBM per device.

v0:
```python
import jax
import jax.numpy as jnp
import numpy as np
from jax import lax
from jax.sharding import PartitionSpec as P

ORDER = 7
CHEB = 4


highest = lax.Precision.HIGHEST
eig_high = 4.0
eig_low = 0.2
gll_inner = np.array(
    [
        -0.8717401485096066,
        -0.5917001814331423,
        -0.20929921790247888,
        0.20929921790247888,
        0.5917001814331423,
        0.8717401485096066,
    ]
)


def padded_2(cells, sides, width):
    for axis, dim in sides:
        count = lax.axis_size(axis)
        ends = count - 1
        head = lax.slice_in_dim(cells, 0, width, axis=dim)
        tail = lax.slice_in_dim(cells, cells.shape[dim] - width, cells.shape[dim], axis=dim)
        cells = jnp.concatenate(
            [
                lax.ppermute(tail, axis, [(i, (i + 1) % count) for i in range(ends)]),
                cells,
                lax.ppermute(head, axis, [((i + 1) % count, i) for i in range(ends)]),
            ],
            axis=dim,
        )
    return cells


def legendre_value(nodes, degree):
    previous = nodes * 0.0 + 1.0
    current = nodes
    for step in range(1, degree):
        following = ((2.0 * step + 1.0) * nodes * current - step * previous) / (step + 1.0)
        previous = current
        current = following
    return current


def gll_tables(poly_order):
    point_count = poly_order + 1
    gll_nodes = np.concatenate([np.array([-1.0]), gll_inner, np.array([1.0])])
    at_nodes = legendre_value(gll_nodes, poly_order)
    weights = 2.0 / (poly_order * point_count * at_nodes**2)
    differences = gll_nodes[:, None] - gll_nodes[None, :] + np.eye(point_count)
    derivative = at_nodes[:, None] / (at_nodes[None, :] * differences) * (1.0 - np.eye(point_count))
    end_value = poly_order * point_count / 4.0
    end_row = np.concatenate(
        [np.array([-end_value]), np.zeros(poly_order - 1), np.array([end_value])]
    )
    derivative = derivative + np.eye(point_count) * end_row[None, :]
    return (derivative, weights)


def forward_parts(field, mats):
    mat_x, mat_y, mat_z = mats
    size_x, size_y, size_z = field.shape
    grad_x = jnp.einsum("ia,ajk->ijk", mat_x, field, precision=highest)
    grad_y = jnp.einsum("ja,iak->ijk", mat_y, field, precision=highest)
    blocks = field.reshape(size_x, size_y, size_z // 128, 128)
    grad_z = jnp.einsum("ca,ijsa->ijsc", mat_z, blocks, precision=highest).reshape(field.shape)
    return (grad_x, grad_y, grad_z)


def backward_sum(parts, mats):
    mat_x, mat_y, mat_z = mats
    part_x, part_y, part_z = parts
    size_x, size_y, size_z = part_x.shape
    total = jnp.einsum("ai,ajk->ijk", mat_x, part_x, precision=highest)
    total = total + jnp.einsum("aj,iak->ijk", mat_y, part_y, precision=highest)
    blocks = part_z.reshape(size_x, size_y, size_z // 128, 128)
    total = total + jnp.einsum("ac,ijsa->ijsc", mat_z, blocks, precision=highest).reshape(
        part_x.shape
    )
    return total


def combine(padded, axis_dim, length, points):
    own = lax.slice_in_dim(padded, 1, length + 1, axis=axis_dim)
    left = lax.slice_in_dim(padded, 0, length, axis=axis_dim)
    right = lax.slice_in_dim(padded, 2, length + 2, axis=axis_dim)
    shape_list = [1, 1, 1]
    shape_list[axis_dim] = length
    position = (jnp.arange(length, dtype=jnp.int32) % points).reshape(shape_list)
    low_mask = (position == 0).astype(jnp.float32)
    high_mask = (position == points - 1).astype(jnp.float32)
    return own + low_mask * left + high_mask * right


def assemble(field, points):
    size_x, size_y, size_z = field.shape
    padded = padded_2(field, (("gx", 0), ("gy", 1), ("gz", 2)), 1)
    summed = combine(padded, 0, size_x, points)
    summed = combine(summed, 1, size_y, points)
    summed = combine(summed, 2, size_z, points)
    return summed


def per_device(right_side, coefficient, agg_weight, coarse_factor):
    points = ORDER + 1
    derivative, weights = gll_tables(ORDER)
    size_x, size_y, size_z = right_side.shape
    mat_x = jnp.asarray(np.kron(np.eye(size_x // points), derivative), dtype=jnp.float32)
    mat_y = jnp.asarray(np.kron(np.eye(size_y // points), derivative), dtype=jnp.float32)
    mat_z = jnp.asarray(np.kron(np.eye(128 // points), derivative), dtype=jnp.float32)
    mats = (mat_x, mat_y, mat_z)
    squares = (mat_x * mat_x, mat_y * mat_y, mat_z * mat_z)
    weight_x = jnp.asarray(np.tile(weights, size_x // points), dtype=jnp.float32)
    weight_y = jnp.asarray(np.tile(weights, size_y // points), dtype=jnp.float32)
    weight_z = jnp.asarray(np.tile(weights, size_z // points), dtype=jnp.float32)
    scaled = (
        coefficient * weight_x[:, None, None] * weight_y[None, :, None] * weight_z[None, None, :]
    )
    diagonal = assemble(backward_sum((scaled, scaled, scaled), squares), points)
    inverse = 1.0 / diagonal
    theta = (eig_high + eig_low) / 2.0
    delta = (eig_high - eig_low) / 2.0
    sigma = theta / delta
    residual = right_side
    direction = inverse * residual / theta
    smoothed = direction
    rho = 1.0 / sigma
    for sweep in range(CHEB):
        grads = forward_parts(direction, mats)
        local = backward_sum((scaled * grads[0], scaled * grads[1], scaled * grads[2]), mats)
        residual = residual - assemble(local, points)
        if sweep + 1 < CHEB:
            rho_new = 1.0 / (2.0 * sigma - rho)
            direction = rho_new * rho * direction + 2.0 * rho_new / delta * inverse * residual
            smoothed = smoothed + direction
            rho = rho_new
    aggregates = coarse_factor.shape[0]
    column_sums = jnp.sum(agg_weight * residual, axis=(0, 1))
    coarse_rhs = jnp.sum(column_sums.reshape(aggregates, size_z // aggregates), axis=1)
    partial_term = jnp.dot(coarse_rhs, coarse_factor, precision=highest)
    projected = lax.psum(partial_term, ("gx", "gy", "gz"))
    coarse_solution = jnp.dot(coarse_factor, projected, precision=highest)
    spread = jnp.repeat(coarse_solution, size_z // aggregates)
    pressure_update = smoothed + agg_weight * spread[None, None, :]
    return (pressure_update, coarse_solution)


def solution(mesh):
    return jax.shard_map(
        per_device,
        mesh=mesh,
        in_specs=(
            P("gx", "gy", "gz"),
            P("gx", "gy", "gz"),
            P("gx", "gy", "gz"),
            P(("gx", "gy", "gz"), None),
        ),
        out_specs=(P("gx", "gy", "gz"), P(("gx", "gy", "gz"))),
        check_vma=False,
    )
```

profile of v0, /device:TPU:0, one launch (start us, length us, event | category | flops | bytes accessed | tf_op | source)
XLA Modules:
  0.0 182.8 jit_solution(2045178090084788073)
XLA Ops:
  4.1 4.8 %collective-permute-start = (f32[1,16,256]{2,0,1:T(1,128)S(1)}, f32[1,16,256]{2,0,1:T(1,128)S(1)}, u32[]{:S(2)}, u32[]{:S(2)}) collective-permute-start(f32[1,16,256]{2,0,1:T(1,128)S(1)} %get-tuple-element.42), channel_id=1, source_target_pairs={{0,16},{1,17},{2,18},{3,19},{4,20},{5,21},{6,22},{7,23},{8,24},{9,... | collective-permute-start | bytes 49160 | tf_op jit(solution)/shard_map/ppermute | solution.py:34
  9.0 1.3 collective-permute-start.1
  10.4 4.2 %collective-permute-done.1 = f32[1,16,256]{2,0,1:T(1,128)S(1)} collective-permute-done((f32[1,16,256]{2,0,1:T(1,128)S(1)}, f32[1,16,256]{2,0,1:T(1,128)S(1)}, u32[]{:S(2)}, u32[]{:S(2)}) %collective-permute-start.1) | collective-permute-done | bytes 16416 | tf_op jit(solution)/shard_map/ppermute | solution.py:36
  15.9 1.3 collective-permute-start.3
  17.2 3.5 %collective-permute-done.3 = f32[10,1,256]{2,0,1:T(8,128)S(1)} collective-permute-done((f32[10,1,256]{2,0,1:T(8,128)S(1)}, f32[10,1,256]{2,0,1:T(8,128)S(1)}, u32[]{:S(2)}, u32[]{:S(2)}) %collective-permute-start.3) | collective-permute-done | bytes 10272 | tf_op jit(solution)/shard_map/ppermute | solution.py:36
  20.9 3.5 %collective-permute-start.4 = (f32[10,18,1]{2,0,1:T(8,128)S(1)}, f32[10,18,1]{2,0,1:T(8,128)S(1)}, u32[]{:S(2)}, u32[]{:S(2)}) collective-permute-start(f32[10,18,1]{2,0,1:T(8,128)S(1)} %get-tuple-element.22), channel_id=1, source_target_pairs={{0,1},{1,2},{2,3},{4,5},{5,6},{6,7},{8,9},{9,10},{10,11},{12,13},{... | collective-permute-start | bytes 2168 | tf_op jit(solution)/shard_map/ppermute | solution.py:34
  24.4 1.3 collective-permute-start.5
  25.7 1.3 collective-permute-done.4
  27.1 4.7 %collective-permute-done.5 = f32[10,18,1]{2,0,1:T(8,128)S(1)} collective-permute-done((f32[10,18,1]{2,0,1:T(8,128)S(1)}, f32[10,18,1]{2,0,1:T(8,128)S(1)}, u32[]{:S(2)}, u32[]{:S(2)}) %collective-permute-start.5) | collective-permute-done | bytes 752 | tf_op jit(solution)/shard_map/ppermute | solution.py:36
  36.7 1.6 collective-permute-start.6
  38.4 1.3 collective-permute-start.7
  39.8 4.2 %collective-permute-done.7 = f32[1,16,256]{2,0,1:T(1,128)S(1)} collective-permute-done((f32[1,16,256]{2,0,1:T(1,128)S(1)}, f32[1,16,256]{2,0,1:T(1,128)S(1)}, u32[]{:S(2)}, u32[]{:S(2)}) %collective-permute-start.7) | collective-permute-done | bytes 16416 | tf_op jit(solution)/shard_map/ppermute | solution.py:36
  44.0 1.5 collective-permute-start.8
  45.6 1.3 collective-permute-start.9
  46.9 3.8 %collective-permute-done.9 = f32[10,1,256]{2,0,1:T(8,128)S(1)} collective-permute-done((f32[10,1,256]{2,0,1:T(8,128)S(1)}, f32[10,1,256]{2,0,1:T(8,128)S(1)}, u32[]{:S(2)}, u32[]{:S(2)}) %collective-permute-start.9) | collective-permute-done | bytes 10272 | tf_op jit(solution)/shard_map/ppermute | solution.py:36
  50.8 3.5 %collective-permute-start.10 = (f32[10,18,1]{2,0,1:T(8,128)S(1)}, f32[10,18,1]{2,0,1:T(8,128)S(1)}, u32[]{:S(2)}, u32[]{:S(2)}) collective-permute-start(f32[10,18,1]{2,0,1:T(8,128)S(1)} %get-tuple-element.20), channel_id=1, source_target_pairs={{0,1},{1,2},{2,3},{4,5},{5,6},{6,7},{8,9},{9,10},{10,11},{12,13},{... | collective-permute-start | bytes 2168 | tf_op jit(solution)/shard_map/ppermute | solution.py:34
  54.3 1.3 collective-permute-start.11
  55.6 1.3 collective-permute-done.10
  57.0 4.7 %collective-permute-done.11 = f32[10,18,1]{2,0,1:T(8,128)S(1)} collective-permute-done((f32[10,18,1]{2,0,1:T(8,128)S(1)}, f32[10,18,1]{2,0,1:T(8,128)S(1)}, u32[]{:S(2)}, u32[]{:S(2)}) %collective-permute-start.11) | collective-permute-done | bytes 752 | tf_op jit(solution)/shard_map/ppermute | solution.py:36
  64.4 1.6 collective-permute-start.12
  66.0 1.3 collective-permute-start.13
  67.4 4.2 %collective-permute-done.13 = f32[1,16,256]{2,0,1:T(1,128)S(1)} collective-permute-done((f32[1,16,256]{2,0,1:T(1,128)S(1)}, f32[1,16,256]{2,0,1:T(1,128)S(1)}, u32[]{:S(2)}, u32[]{:S(2)}) %collective-permute-start.13) | collective-permute-done | bytes 16416 | tf_op jit(solution)/shard_map/ppermute | solution.py:36
  71.7 1.5 collective-permute-start.14
  73.2 1.3 collective-permute-start.15
  74.5 3.8 %collective-permute-done.15 = f32[10,1,256]{2,0,1:T(8,128)S(1)} collective-permute-done((f32[10,1,256]{2,0,1:T(8,128)S(1)}, f32[10,1,256]{2,0,1:T(8,128)S(1)}, u32[]{:S(2)}, u32[]{:S(2)}) %collective-permute-start.15) | collective-permute-done | bytes 10272 | tf_op jit(solution)/shard_map/ppermute | solution.py:36
  78.5 3.5 %collective-permute-start.16 = (f32[10,18,1]{2,0,1:T(8,128)S(1)}, f32[10,18,1]{2,0,1:T(8,128)S(1)}, u32[]{:S(2)}, u32[]{:S(2)}) collective-permute-start(f32[10,18,1]{2,0,1:T(8,128)S(1)} %get-tuple-element.18), channel_id=1, source_target_pairs={{0,1},{1,2},{2,3},{4,5},{5,6},{6,7},{8,9},{9,10},{10,11},{12,13},{... | collective-permute-start | bytes 2168 | tf_op jit(solution)/shard_map/ppermute | solution.py:34
  82.0 1.3 collective-permute-start.17
  83.3 1.3 collective-permute-done.16
  84.6 4.7 %collective-permute-done.17 = f32[10,18,1]{2,0,1:T(8,128)S(1)} collective-permute-done((f32[10,18,1]{2,0,1:T(8,128)S(1)}, f32[10,18,1]{2,0,1:T(8,128)S(1)}, u32[]{:S(2)}, u32[]{:S(2)}) %collective-permute-start.17) | collective-permute-done | bytes 752 | tf_op jit(solution)/shard_map/ppermute | solution.py:36
  92.1 1.6 collective-permute-start.18
  93.7 1.3 collective-permute-start.19
  95.2 4.2 %collective-permute-done.19 = f32[1,16,256]{2,0,1:T(1,128)S(1)} collective-permute-done((f32[1,16,256]{2,0,1:T(1,128)S(1)}, f32[1,16,256]{2,0,1:T(1,128)S(1)}, u32[]{:S(2)}, u32[]{:S(2)}) %collective-permute-start.19) | collective-permute-done | bytes 16416 | tf_op jit(solution)/shard_map/ppermute | solution.py:36
  99.4 1.5 collective-permute-start.20
  100.9 1.3 collective-permute-start.21
  102.3 3.8 %collective-permute-done.21 = f32[10,1,256]{2,0,1:T(8,128)S(1)} collective-permute-done((f32[10,1,256]{2,0,1:T(8,128)S(1)}, f32[10,1,256]{2,0,1:T(8,128)S(1)}, u32[]{:S(2)}, u32[]{:S(2)}) %collective-permute-start.21) | collective-permute-done | bytes 10272 | tf_op jit(solution)/shard_map/ppermute | solution.py:36
  106.2 1.9 %collective-permute-start.22 = (f32[10,18,1]{2,0,1:T(8,128)S(1)}, f32[10,18,1]{2,0,1:T(8,128)S(1)}, u32[]{:S(2)}, u32[]{:S(2)}) collective-permute-start(f32[10,18,1]{2,0,1:T(8,128)S(1)} %get-tuple-element.16), channel_id=1, source_target_pairs={{0,1},{1,2},{2,3},{4,5},{5,6},{6,7},{8,9},{9,10},{10,11},{12,13},{... | collective-permute-start | bytes 2168 | tf_op jit(solution)/shard_map/ppermute | solution.py:34
  108.1 1.3 collective-permute-start.23
  109.4 1.3 collective-permute-done.22
  110.8 4.7 %collective-permute-done.23 = f32[10,18,1]{2,0,1:T(8,128)S(1)} collective-permute-done((f32[10,18,1]{2,0,1:T(8,128)S(1)}, f32[10,18,1]{2,0,1:T(8,128)S(1)}, u32[]{:S(2)}, u32[]{:S(2)}) %collective-permute-start.23) | collective-permute-done | bytes 752 | tf_op jit(solution)/shard_map/ppermute | solution.py:36
  118.2 1.6 collective-permute-start.24
  121.2 4.2 %collective-permute-done.25 = f32[1,16,256]{2,0,1:T(1,128)S(1)} collective-permute-done((f32[1,16,256]{2,0,1:T(1,128)S(1)}, f32[1,16,256]{2,0,1:T(1,128)S(1)}, u32[]{:S(2)}, u32[]{:S(2)}) %collective-permute-start.25) | collective-permute-done | bytes 16416 | tf_op jit(solution)/shard_map/ppermute | solution.py:36
  125.5 1.8 %collective-permute-start.26 = (f32[10,1,256]{2,0,1:T(8,128)S(1)}, f32[10,1,256]{2,0,1:T(8,128)S(1)}, u32[]{:S(2)}, u32[]{:S(2)}) collective-permute-start(f32[10,1,256]{2,0,1:T(8,128)S(1)} %get-tuple-element.24), channel_id=1, source_target_pairs={{0,4},{4,8},{8,12},{1,5},{5,9},{9,13},{2,6},{6,10},{10,14},{3,7},{... | collective-permute-start | bytes 30728 | tf_op jit(solution)/shard_map/ppermute | solution.py:34
  128.6 3.5 %collective-permute-done.27 = f32[10,1,256]{2,0,1:T(8,128)S(1)} collective-permute-done((f32[10,1,256]{2,0,1:T(8,128)S(1)}, f32[10,1,256]{2,0,1:T(8,128)S(1)}, u32[]{:S(2)}, u32[]{:S(2)}) %collective-permute-start.27) | collective-permute-done | bytes 10272 | tf_op jit(solution)/shard_map/ppermute | solution.py:36
  132.3 1.9 %collective-permute-start.28 = (f32[10,18,1]{2,0,1:T(8,128)S(1)}, f32[10,18,1]{2,0,1:T(8,128)S(1)}, u32[]{:S(2)}, u32[]{:S(2)}) collective-permute-start(f32[10,18,1]{2,0,1:T(8,128)S(1)} %get-tuple-element.14), channel_id=1, source_target_pairs={{0,1},{1,2},{2,3},{4,5},{5,6},{6,7},{8,9},{9,10},{10,11},{12,13},{... | collective-permute-start | bytes 2168 | tf_op jit(solution)/shard_map/ppermute | solution.py:34
  134.2 1.3 collective-permute-start.29
  135.5 1.3 collective-permute-done.28
  136.9 4.7 %collective-permute-done.29 = f32[10,18,1]{2,0,1:T(8,128)S(1)} collective-permute-done((f32[10,18,1]{2,0,1:T(8,128)S(1)}, f32[10,18,1]{2,0,1:T(8,128)S(1)}, u32[]{:S(2)}, u32[]{:S(2)}) %collective-permute-start.29) | collective-permute-done | bytes 752 | tf_op jit(solution)/shard_map/ppermute | solution.py:36
  143.4 37.8 %psum.7 = f32[256]{0:T(256)S(1)} all-reduce(f32[256]{0:T(256)S(1)} %bitcast.142), channel_id=1, replica_groups=mesh['gx'=2,'gy'=4,'gz'=4] {'gx','gy','gz'}, use_global_device_ids=true, to_apply=%region_2.3 | all-reduce | flops 256 | bytes 2048 | tf_op jit(solution)/shard_map/psum | solution.py:149
  (124 shorter events, 24.7 us)
Async XLA Ops:
  0.6 142.7 %copy-start = (f32[8,256]{1,0:T(8,128)S(1)}, f32[8,256]{1,0:T(8,128)}, u32[]{:S(2)}) copy-start(f32[8,256]{1,0:T(8,128)} %param.13) | copy-start | bytes 24580
  0.6 0.7 copy-start.9
  0.7 0.7 copy-start.7
  0.7 0.7 copy-start.8
  0.7 1.7 copy-start.10
  0.7 1.7 copy-start.1
  2.4 0.7 copy-start.11
  3.1 0.7 copy-start.12
  4.1 6.3 %collective-permute-start = (f32[1,16,256]{2,0,1:T(1,128)S(1)}, f32[1,16,256]{2,0,1:T(1,128)S(1)}, u32[]{:S(2)}, u32[]{:S(2)}) collective-permute-start(f32[1,16,256]{2,0,1:T(1,128)S(1)} %get-tuple-element.42), channel_id=1, source_target_pairs={{0,16},{1,17},{2,18},{3,19},{4,20},{5,21},{6,22},{7,23},{8,24},{9,... | collective-permute-start | bytes 49160 | tf_op jit(solution)/shard_map/ppermute | solution.py:34
  9.0 5.6 %collective-permute-start.1 = (f32[1,16,256]{2,0,1:T(1,128)S(1)}, f32[1,16,256]{2,0,1:T(1,128)S(1)}, u32[]{:S(2)}, u32[]{:S(2)}) collective-permute-start(f32[1,16,256]{2,0,1:T(1,128)S(1)} %get-tuple-element.43), channel_id=1, source_target_pairs={{16,0},{17,1},{18,2},{19,3},{20,4},{21,5},{22,6},{23,7},{24,8},{25... | collective-permute-start | bytes 49160 | tf_op jit(solution)/shard_map/ppermute | solution.py:36
  14.6 2.6 %collective-permute-start.2 = (f32[10,1,256]{2,0,1:T(8,128)S(1)}, f32[10,1,256]{2,0,1:T(8,128)S(1)}, u32[]{:S(2)}, u32[]{:S(2)}) collective-permute-start(f32[10,1,256]{2,0,1:T(8,128)S(1)} %get-tuple-element.32), channel_id=1, source_target_pairs={{0,4},{4,8},{8,12},{1,5},{5,9},{9,13},{2,6},{6,10},{10,14},{3,7},{... | collective-permute-start | bytes 30728 | tf_op jit(solution)/shard_map/ppermute | solution.py:34
  15.9 4.8 %collective-permute-start.3 = (f32[10,1,256]{2,0,1:T(8,128)S(1)}, f32[10,1,256]{2,0,1:T(8,128)S(1)}, u32[]{:S(2)}, u32[]{:S(2)}) collective-permute-start(f32[10,1,256]{2,0,1:T(8,128)S(1)} %get-tuple-element.33), channel_id=1, source_target_pairs={{4,0},{8,4},{12,8},{5,1},{9,5},{13,9},{6,2},{10,6},{14,10},{7,3},{... | collective-permute-start | bytes 30728 | tf_op jit(solution)/shard_map/ppermute | solution.py:36
  20.9 6.1 %collective-permute-start.4 = (f32[10,18,1]{2,0,1:T(8,128)S(1)}, f32[10,18,1]{2,0,1:T(8,128)S(1)}, u32[]{:S(2)}, u32[]{:S(2)}) collective-permute-start(f32[10,18,1]{2,0,1:T(8,128)S(1)} %get-tuple-element.22), channel_id=1, source_target_pairs={{0,1},{1,2},{2,3},{4,5},{5,6},{6,7},{8,9},{9,10},{10,11},{12,13},{... | collective-permute-start | bytes 2168 | tf_op jit(solution)/shard_map/ppermute | solution.py:34
  24.4 7.4 %collective-permute-start.5 = (f32[10,18,1]{2,0,1:T(8,128)S(1)}, f32[10,18,1]{2,0,1:T(8,128)S(1)}, u32[]{:S(2)}, u32[]{:S(2)}) collective-permute-start(f32[10,18,1]{2,0,1:T(8,128)S(1)} %get-tuple-element.23), channel_id=1, source_target_pairs={{1,0},{2,1},{3,2},{5,4},{6,5},{7,6},{9,8},{10,9},{11,10},{13,12},{... | collective-permute-start | bytes 2168 | tf_op jit(solution)/shard_map/ppermute | solution.py:36
  32.2 0.9 copy-start.3
  33.1 0.8 copy-start.2
  34.3 0.7 copy-start.4
  35.4 0.7 copy-start.6
  36.7 3.1 %collective-permute-start.6 = (f32[1,16,256]{2,0,1:T(1,128)S(1)}, f32[1,16,256]{2,0,1:T(1,128)S(1)}, u32[]{:S(2)}, u32[]{:S(2)}) collective-permute-start(f32[1,16,256]{2,0,1:T(1,128)S(1)} %get-tuple-element.40), channel_id=1, source_target_pairs={{0,16},{1,17},{2,18},{3,19},{4,20},{5,21},{6,22},{7,23},{8,24},{9,... | collective-permute-start | bytes 49160 | tf_op jit(solution)/shard_map/ppermute | solution.py:34
  38.4 5.6 %collective-permute-start.7 = (f32[1,16,256]{2,0,1:T(1,128)S(1)}, f32[1,16,256]{2,0,1:T(1,128)S(1)}, u32[]{:S(2)}, u32[]{:S(2)}) collective-permute-start(f32[1,16,256]{2,0,1:T(1,128)S(1)} %get-tuple-element.41), channel_id=1, source_target_pairs={{16,0},{17,1},{18,2},{19,3},{20,4},{21,5},{22,6},{23,7},{24,8},{25... | collective-permute-start | bytes 49160 | tf_op jit(solution)/shard_map/ppermute | solution.py:36
  44.0 2.9 %collective-permute-start.8 = (f32[10,1,256]{2,0,1:T(8,128)S(1)}, f32[10,1,256]{2,0,1:T(8,128)S(1)}, u32[]{:S(2)}, u32[]{:S(2)}) collective-permute-start(f32[10,1,256]{2,0,1:T(8,128)S(1)} %get-tuple-element.30), channel_id=1, source_target_pairs={{0,4},{4,8},{8,12},{1,5},{5,9},{9,13},{2,6},{6,10},{10,14},{3,7},{... | collective-permute-start | bytes 30728 | tf_op jit(solution)/shard_map/ppermute | solution.py:34
  45.6 5.1 %collective-permute-start.9 = (f32[10,1,256]{2,0,1:T(8,128)S(1)}, f32[10,1,256]{2,0,1:T(8,128)S(1)}, u32[]{:S(2)}, u32[]{:S(2)}) collective-permute-start(f32[10,1,256]{2,0,1:T(8,128)S(1)} %get-tuple-element.31), channel_id=1, source_target_pairs={{4,0},{8,4},{12,8},{5,1},{9,5},{13,9},{6,2},{10,6},{14,10},{7,3},{... | collective-permute-start | bytes 30728 | tf_op jit(solution)/shard_map/ppermute | solution.py:36
  50.8 6.1 %collective-permute-start.10 = (f32[10,18,1]{2,0,1:T(8,128)S(1)}, f32[10,18,1]{2,0,1:T(8,128)S(1)}, u32[]{:S(2)}, u32[]{:S(2)}) collective-permute-start(f32[10,18,1]{2,0,1:T(8,128)S(1)} %get-tuple-element.20), channel_id=1, source_target_pairs={{0,1},{1,2},{2,3},{4,5},{5,6},{6,7},{8,9},{9,10},{10,11},{12,13},{... | collective-permute-start | bytes 2168 | tf_op jit(solution)/shard_map/ppermute | solution.py:34
  54.3 7.4 %collective-permute-start.11 = (f32[10,18,1]{2,0,1:T(8,128)S(1)}, f32[10,18,1]{2,0,1:T(8,128)S(1)}, u32[]{:S(2)}, u32[]{:S(2)}) collective-permute-start(f32[10,18,1]{2,0,1:T(8,128)S(1)} %get-tuple-element.21), channel_id=1, source_target_pairs={{1,0},{2,1},{3,2},{5,4},{6,5},{7,6},{9,8},{10,9},{11,10},{13,12},{... | collective-permute-start | bytes 2168 | tf_op jit(solution)/shard_map/ppermute | solution.py:36
  64.4 3.1 %collective-permute-start.12 = (f32[1,16,256]{2,0,1:T(1,128)S(1)}, f32[1,16,256]{2,0,1:T(1,128)S(1)}, u32[]{:S(2)}, u32[]{:S(2)}) collective-permute-start(f32[1,16,256]{2,0,1:T(1,128)S(1)} %get-tuple-element.38), channel_id=1, source_target_pairs={{0,16},{1,17},{2,18},{3,19},{4,20},{5,21},{6,22},{7,23},{8,24},{9,... | collective-permute-start | bytes 49160 | tf_op jit(solution)/shard_map/ppermute | solution.py:34
  66.0 5.6 %collective-permute-start.13 = (f32[1,16,256]{2,0,1:T(1,128)S(1)}, f32[1,16,256]{2,0,1:T(1,128)S(1)}, u32[]{:S(2)}, u32[]{:S(2)}) collective-permute-start(f32[1,16,256]{2,0,1:T(1,128)S(1)} %get-tuple-element.39), channel_id=1, source_target_pairs={{16,0},{17,1},{18,2},{19,3},{20,4},{21,5},{22,6},{23,7},{24,8},{25... | collective-permute-start | bytes 49160 | tf_op jit(solution)/shard_map/ppermute | solution.py:36
  71.7 2.9 %collective-permute-start.14 = (f32[10,1,256]{2,0,1:T(8,128)S(1)}, f32[10,1,256]{2,0,1:T(8,128)S(1)}, u32[]{:S(2)}, u32[]{:S(2)}) collective-permute-start(f32[10,1,256]{2,0,1:T(8,128)S(1)} %get-tuple-element.28), channel_id=1, source_target_pairs={{0,4},{4,8},{8,12},{1,5},{5,9},{9,13},{2,6},{6,10},{10,14},{3,7},{... | collective-permute-start | bytes 30728 | tf_op jit(solution)/shard_map/ppermute | solution.py:34
  73.2 5.1 %collective-permute-start.15 = (f32[10,1,256]{2,0,1:T(8,128)S(1)}, f32[10,1,256]{2,0,1:T(8,128)S(1)}, u32[]{:S(2)}, u32[]{:S(2)}) collective-permute-start(f32[10,1,256]{2,0,1:T(8,128)S(1)} %get-tuple-element.29), channel_id=1, source_target_pairs={{4,0},{8,4},{12,8},{5,1},{9,5},{13,9},{6,2},{10,6},{14,10},{7,3},{... | collective-permute-start | bytes 30728 | tf_op jit(solution)/shard_map/ppermute | solution.py:36
  78.5 6.1 %collective-permute-start.16 = (f32[10,18,1]{2,0,1:T(8,128)S(1)}, f32[10,18,1]{2,0,1:T(8,128)S(1)}, u32[]{:S(2)}, u32[]{:S(2)}) collective-permute-start(f32[10,18,1]{2,0,1:T(8,128)S(1)} %get-tuple-element.18), channel_id=1, source_target_pairs={{0,1},{1,2},{2,3},{4,5},{5,6},{6,7},{8,9},{9,10},{10,11},{12,13},{... | collective-permute-start | bytes 2168 | tf_op jit(solution)/shard_map/ppermute | solution.py:34
  82.0 7.4 %collective-permute-start.17 = (f32[10,18,1]{2,0,1:T(8,128)S(1)}, f32[10,18,1]{2,0,1:T(8,128)S(1)}, u32[]{:S(2)}, u32[]{:S(2)}) collective-permute-start(f32[10,18,1]{2,0,1:T(8,128)S(1)} %get-tuple-element.19), channel_id=1, source_target_pairs={{1,0},{2,1},{3,2},{5,4},{6,5},{7,6},{9,8},{10,9},{11,10},{13,12},{... | collective-permute-start | bytes 2168 | tf_op jit(solution)/shard_map/ppermute | solution.py:36
  92.1 3.1 %collective-permute-start.18 = (f32[1,16,256]{2,0,1:T(1,128)S(1)}, f32[1,16,256]{2,0,1:T(1,128)S(1)}, u32[]{:S(2)}, u32[]{:S(2)}) collective-permute-start(f32[1,16,256]{2,0,1:T(1,128)S(1)} %get-tuple-element.36), channel_id=1, source_target_pairs={{0,16},{1,17},{2,18},{3,19},{4,20},{5,21},{6,22},{7,23},{8,24},{9,... | collective-permute-start | bytes 49160 | tf_op jit(solution)/shard_map/ppermute | solution.py:34
  93.7 5.6 %collective-permute-start.19 = (f32[1,16,256]{2,0,1:T(1,128)S(1)}, f32[1,16,256]{2,0,1:T(1,128)S(1)}, u32[]{:S(2)}, u32[]{:S(2)}) collective-permute-start(f32[1,16,256]{2,0,1:T(1,128)S(1)} %get-tuple-element.37), channel_id=1, source_target_pairs={{16,0},{17,1},{18,2},{19,3},{20,4},{21,5},{22,6},{23,7},{24,8},{25... | collective-permute-start | bytes 49160 | tf_op jit(solution)/shard_map/ppermute | solution.py:36
  99.4 2.9 %collective-permute-start.20 = (f32[10,1,256]{2,0,1:T(8,128)S(1)}, f32[10,1,256]{2,0,1:T(8,128)S(1)}, u32[]{:S(2)}, u32[]{:S(2)}) collective-permute-start(f32[10,1,256]{2,0,1:T(8,128)S(1)} %get-tuple-element.26), channel_id=1, source_target_pairs={{0,4},{4,8},{8,12},{1,5},{5,9},{9,13},{2,6},{6,10},{10,14},{3,7},{... | collective-permute-start | bytes 30728 | tf_op jit(solution)/shard_map/ppermute | solution.py:34
  100.9 5.1 %collective-permute-start.21 = (f32[10,1,256]{2,0,1:T(8,128)S(1)}, f32[10,1,256]{2,0,1:T(8,128)S(1)}, u32[]{:S(2)}, u32[]{:S(2)}) collective-permute-start(f32[10,1,256]{2,0,1:T(8,128)S(1)} %get-tuple-element.27), channel_id=1, source_target_pairs={{4,0},{8,4},{12,8},{5,1},{9,5},{13,9},{6,2},{10,6},{14,10},{7,3},{... | collective-permute-start | bytes 30728 | tf_op jit(solution)/shard_map/ppermute | solution.py:36
  106.2 4.6 %collective-permute-start.22 = (f32[10,18,1]{2,0,1:T(8,128)S(1)}, f32[10,18,1]{2,0,1:T(8,128)S(1)}, u32[]{:S(2)}, u32[]{:S(2)}) collective-permute-start(f32[10,18,1]{2,0,1:T(8,128)S(1)} %get-tuple-element.16), channel_id=1, source_target_pairs={{0,1},{1,2},{2,3},{4,5},{5,6},{6,7},{8,9},{9,10},{10,11},{12,13},{... | collective-permute-start | bytes 2168 | tf_op jit(solution)/shard_map/ppermute | solution.py:34
  108.1 7.4 %collective-permute-start.23 = (f32[10,18,1]{2,0,1:T(8,128)S(1)}, f32[10,18,1]{2,0,1:T(8,128)S(1)}, u32[]{:S(2)}, u32[]{:S(2)}) collective-permute-start(f32[10,18,1]{2,0,1:T(8,128)S(1)} %get-tuple-element.17), channel_id=1, source_target_pairs={{1,0},{2,1},{3,2},{5,4},{6,5},{7,6},{9,8},{10,9},{11,10},{13,12},{... | collective-permute-start | bytes 2168 | tf_op jit(solution)/shard_map/ppermute | solution.py:36
  118.2 3.1 %collective-permute-start.24 = (f32[1,16,256]{2,0,1:T(1,128)S(1)}, f32[1,16,256]{2,0,1:T(1,128)S(1)}, u32[]{:S(2)}, u32[]{:S(2)}) collective-permute-start(f32[1,16,256]{2,0,1:T(1,128)S(1)} %get-tuple-element.34), channel_id=1, source_target_pairs={{0,16},{1,17},{2,18},{3,19},{4,20},{5,21},{6,22},{7,23},{8,24},{9,... | collective-permute-start | bytes 49160 | tf_op jit(solution)/shard_map/ppermute | solution.py:34
  119.8 5.6 %collective-permute-start.25 = (f32[1,16,256]{2,0,1:T(1,128)S(1)}, f32[1,16,256]{2,0,1:T(1,128)S(1)}, u32[]{:S(2)}, u32[]{:S(2)}) collective-permute-start(f32[1,16,256]{2,0,1:T(1,128)S(1)} %get-tuple-element.35), channel_id=1, source_target_pairs={{16,0},{17,1},{18,2},{19,3},{20,4},{21,5},{22,6},{23,7},{24,8},{25... | collective-permute-start | bytes 49160 | tf_op jit(solution)/shard_map/ppermute | solution.py:36
  125.5 3.2 %collective-permute-start.26 = (f32[10,1,256]{2,0,1:T(8,128)S(1)}, f32[10,1,256]{2,0,1:T(8,128)S(1)}, u32[]{:S(2)}, u32[]{:S(2)}) collective-permute-start(f32[10,1,256]{2,0,1:T(8,128)S(1)} %get-tuple-element.24), channel_id=1, source_target_pairs={{0,4},{4,8},{8,12},{1,5},{5,9},{9,13},{2,6},{6,10},{10,14},{3,7},{... | collective-permute-start | bytes 30728 | tf_op jit(solution)/shard_map/ppermute | solution.py:34
  127.3 4.8 %collective-permute-start.27 = (f32[10,1,256]{2,0,1:T(8,128)S(1)}, f32[10,1,256]{2,0,1:T(8,128)S(1)}, u32[]{:S(2)}, u32[]{:S(2)}) collective-permute-start(f32[10,1,256]{2,0,1:T(8,128)S(1)} %get-tuple-element.25), channel_id=1, source_target_pairs={{4,0},{8,4},{12,8},{5,1},{9,5},{13,9},{6,2},{10,6},{14,10},{7,3},{... | collective-permute-start | bytes 30728 | tf_op jit(solution)/shard_map/ppermute | solution.py:36
  132.3 4.6 %collective-permute-start.28 = (f32[10,18,1]{2,0,1:T(8,128)S(1)}, f32[10,18,1]{2,0,1:T(8,128)S(1)}, u32[]{:S(2)}, u32[]{:S(2)}) collective-permute-start(f32[10,18,1]{2,0,1:T(8,128)S(1)} %get-tuple-element.14), channel_id=1, source_target_pairs={{0,1},{1,2},{2,3},{4,5},{5,6},{6,7},{8,9},{9,10},{10,11},{12,13},{... | collective-permute-start | bytes 2168 | tf_op jit(solution)/shard_map/ppermute | solution.py:34
  134.2 7.4 %collective-permute-start.29 = (f32[10,18,1]{2,0,1:T(8,128)S(1)}, f32[10,18,1]{2,0,1:T(8,128)S(1)}, u32[]{:S(2)}, u32[]{:S(2)}) collective-permute-start(f32[10,18,1]{2,0,1:T(8,128)S(1)} %get-tuple-element.15), channel_id=1, source_target_pairs={{1,0},{2,1},{3,2},{5,4},{6,5},{7,6},{9,8},{10,9},{11,10},{13,12},{... | collective-permute-start | bytes 2168 | tf_op jit(solution)/shard_map/ppermute | solution.py:36
  142.0 0.9 copy-start.5
  181.4 0.5 copy-start.13
where the time goes:
time: 184 us; the launch traced here: 183 us
  waiting for transfers between devices  70.4 us (38%)
  starting transfers between devices  52.9 us (29%)
  blocking collectives  37.8 us (21%)
  matrix products  8.03 us (4%)
  local copies, waits for them, and re-layouts  6.47 us (4%)
  other arithmetic  5.7 us (3%)
    ppermute x15, waiting for transfers between devices, padded_2(): lax.ppermute(head, axis, [((i + 1) % count, i) for i in range(ends)])  63 us
    psum x1, blocking collectives, per_device(): projected = lax.psum(partial_term, ('gx', 'gy', 'gz'))  37.8 us
    ppermute x15, starting transfers between devices, padded_2(): lax.ppermute(tail, axis, [(i, (i + 1) % count) for i in range(ends)])  33.5 us
    ppermute x15, starting transfers between devices, padded_2(): lax.ppermute(head, axis, [((i + 1) % count, i) for i in range(ends)])  19.4 us
    ppermute x15, waiting for transfers between devices, padded_2(): lax.ppermute(tail, axis, [(i, (i + 1) % count) for i in range(ends)])  7.36 us
    unnamed x29, local copies, waits for them, and re-layouts  5.65 us
  transfers between devices with their start and end apart: 30, of which 25 were waited for; matrix products, arithmetic and copies ran while one was open for 0% of the time, Pallas kernels for 0%

commit v1 on v0

v1 whole, which is shorter than its diff:
```python
import functools
import itertools

import jax
import jax.numpy as jnp
import ml_dtypes
import numpy as np
from jax import lax
from jax.experimental import pallas as pl
from jax.experimental.pallas import tpu as pltpu
from jax.sharding import PartitionSpec as P

ORDER = 7
CHEB = 4
MESH = pl.DeviceIdType.MESH
eig_high = 4.0
eig_low = 0.2
gll_inner = np.array(
    [
        -0.8717401485096066,
        -0.5917001814331423,
        -0.20929921790247888,
        0.20929921790247888,
        0.5917001814331423,
        0.8717401485096066,
    ]
)


def legendre_value(nodes, degree):
    previous = nodes * 0.0 + 1.0
    current = nodes
    for step in range(1, degree):
        following = ((2.0 * step + 1.0) * nodes * current - step * previous) / (step + 1.0)
        previous = current
        current = following
    return current


def gll_tables(poly_order):
    point_count = poly_order + 1
    gll_nodes = np.concatenate([np.array([-1.0]), gll_inner, np.array([1.0])])
    at_nodes = legendre_value(gll_nodes, poly_order)
    weights = 2.0 / (poly_order * point_count * at_nodes**2)
    differences = gll_nodes[:, None] - gll_nodes[None, :] + np.eye(point_count)
    derivative = at_nodes[:, None] / (at_nodes[None, :] * differences) * (1.0 - np.eye(point_count))
    end_value = poly_order * point_count / 4.0
    end_row = np.concatenate(
        [np.array([-end_value]), np.zeros(poly_order - 1), np.array([end_value])]
    )
    derivative = derivative + np.eye(point_count) * end_row[None, :]
    return (derivative, weights)


def halves(matrix):
    full = np.asarray(matrix, np.float32)
    high = full.astype(ml_dtypes.bfloat16)
    low = (full - high.astype(np.float32)).astype(ml_dtypes.bfloat16)
    return np.stack([high, low])


def tables(size_x, size_y, size_z):
    points = ORDER + 1
    derivative, weights = gll_tables(ORDER)
    derivative = derivative.astype(np.float32)
    squared = derivative * derivative
    ex, ey, ez = size_x // points, size_y // points, size_z // points

    def along_x(m):
        return np.kron(np.kron(np.eye(ex), m), np.eye(size_y))

    def along_y(m):
        return np.kron(np.eye(size_x), np.kron(np.eye(ey), m))

    def along_z(m):
        return np.kron(np.eye(ez), m)

    forward = np.concatenate([along_x(derivative), along_y(derivative)], axis=0)
    weights = weights.astype(np.float32)
    w_xy = np.kron(np.tile(weights, ex), np.tile(weights, ey))
    quad = (w_xy[:, None] * np.tile(weights, ez)[None, :]).astype(np.float32)
    return (
        quad,
        halves(along_x(squared.T) + along_y(squared.T)),
        halves(along_z(squared)),
        halves(forward),
        halves(along_z(derivative.T)),
        halves(forward.T),
        halves(along_z(derivative)),
    )


def split(value):
    high = value.astype(jnp.bfloat16)
    low = (value - high.astype(jnp.float32)).astype(jnp.bfloat16)
    return high, low


def dot(a, b):
    return jnp.dot(a, b, preferred_element_type=jnp.float32)


def from_left(mat, value):
    high, low = split(value)
    return dot(mat[0], high) + (dot(mat[0], low) + dot(mat[1], high))


def from_right(value, mat):
    high, low = split(value)
    return dot(high, mat[0]) + (dot(low, mat[0]) + dot(high, mat[1]))


def kernel(dims, sizes, *refs):
    gx, gy, gz = dims
    sx, sy, sz = sizes
    rows = sx * sy
    inputs, (out, out_c), scratch = refs[:11], refs[11:13], refs[13:]
    held, (field, yface, zface, xr, yr, er, zr, part, got1, got2), sems = (
        scratch[:11],
        scratch[11:21],
        scratch[21:],
    )
    in_sem, send_sem, recv_sem, send1, recv1, send2, recv2 = sems
    ix, iy, iz = (lax.axis_index(a) for a in ("gx", "gy", "gz"))

    loads = [pltpu.make_async_copy(i, h, in_sem.at[k]) for k, (i, h) in enumerate(zip(inputs, held))]
    for load in loads:
        load.start()
    coef, rhs, agg, factor, quad, sq_xy, sq_z, f_xy, f_z, b_xy, b_z = held

    for buf in (xr, yr, er, zr):
        buf[...] = jnp.zeros_like(buf)

    def options(index, count):
        if count == 1:
            return [(0, None)]
        if count == 2:
            return [(0, None), (1 - 2 * index, None)]
        return [(0, None), (1, index < count - 1), (-1, index > 0)]

    def around():
        for (dx, cx), (dy, cy), (dz, cz) in itertools.product(
            options(ix, gx), options(iy, gy), options(iz, gz)
        ):
            zero = [isinstance(d, int) and d == 0 for d in (dx, dy, dz)]
            if all(zero):
                continue
            conds = [c for c in (cx, cy, cz) if c is not None]
            cond = None
            for c in conds:
                cond = c if cond is None else jnp.logical_and(cond, c)
            yield (dx, dy, dz), zero, cond

    def guarded(cond, action):
        if cond is None:
            action()
        else:
            pl.when(cond)(action)

    nxy = gx * gy
    me_xy = ix * gy + iy
    peers1 = []
    for j in range(1, nxy):
        other = lax.rem(me_xy + j, nxy)
        peers1.append((other // gy, lax.rem(other, gy), iz))
    peers2 = [(ix, iy, lax.rem(iz + j, gz)) for j in range(1, gz)]

    barrier = pltpu.get_barrier_semaphore()
    for offset, _, cond in around():
        def greet(offset=offset):
            pl.semaphore_signal(
                barrier,
                inc=1,
                device_id=(ix + offset[0], iy + offset[1], iz + offset[2]),
                device_id_type=MESH,
            )

        guarded(cond, greet)
    for peer in peers1 + peers2:
        pl.semaphore_signal(barrier, inc=1, device_id=peer, device_id_type=MESH)

    def present(index, count):
        if count <= 2:
            return count
        return 3 - (index == 0).astype(jnp.int32) - (index == count - 1).astype(jnp.int32)

    greeted = present(ix, gx) * present(iy, gy) * present(iz, gz) - 1 + len(peers1) + len(peers2)

    def message(slot, offset, zero):
        dx, dy, dz = offset
        mark = (1 - dx) * 9 + (1 - dy) * 3 + (1 - dz)
        low_x, low_y, low_z = [(1 + d) // 2 for d in offset]
        if not zero[2]:
            src = zface.at[slot, low_z]
            dst = zr.at[slot, 1 - low_z, (1 - dx) * 3 + (1 - dy)]
        elif not zero[1] and not zero[0]:
            src = yface.at[slot, low_y]
            dst = er.at[slot, (1 - low_x) * 2 + (1 - low_y)]
        elif not zero[1]:
            src = yface.at[slot, low_y]
            dst = yr.at[slot, 1 - low_y]
        else:
            src = field.at[slot, pl.ds(pl.multiple_of(low_x * (rows - sy), sy), sy)]
            dst = xr.at[slot, 1 - low_x]
        return pltpu.make_async_remote_copy(
            src_ref=src,
            dst_ref=dst,
            send_sem=send_sem.at[slot, mark],
            recv_sem=recv_sem.at[slot, mark],
            device_id=(ix + dx, iy + dy, iz + dz),
            device_id_type=MESH,
        )

    def incoming(slot, offset, zero):
        return message(slot, tuple(-d for d in offset), zero)

    row = lax.broadcasted_iota(jnp.int32, (rows, sz), 0)
    lane = lax.broadcasted_iota(jnp.int32, (rows, sz), 1)
    y_at = lax.rem(row, sy)
    y_node = lax.rem(row, 8)
    z_node = lax.rem(lane, 8)
    x_of = lax.broadcasted_iota(jnp.int32, (sx, sz), 0)
    p_lane = lax.broadcasted_iota(jnp.int32, (8, rows), 1)
    p_y = lax.rem(p_lane, sy)
    lane_half = lax.broadcasted_iota(jnp.int32, (rows, 128), 1)

    def plane(slot, side):
        def summed_x(b):
            own = zr[slot, side, 3 + b]
            low = jnp.where(p_lane < sy, pltpu.roll(zr[slot, side, b], sy, 1), 0.0)
            high = jnp.where(
                p_lane >= rows - sy, pltpu.roll(zr[slot, side, 6 + b], rows - sy, 1), 0.0
            )
            return own + low + high

        before, mine, after = summed_x(0), summed_x(1), summed_x(2)
        low = jnp.where(
            p_y == 0, pltpu.roll(before, rows - (sy - 1), 1), pltpu.roll(mine, 1, 1)
        )
        high = jnp.where(
            p_y == sy - 1, pltpu.roll(after, sy - 1, 1), pltpu.roll(mine, rows - 1, 1)
        )
        node = lax.rem(p_lane, 8)
        return mine + jnp.where(node == 0, low, 0.0) + jnp.where(node == 7, high, 0.0)

    def assemble(slot, local):
        field[slot] = local
        cube = local.reshape(sx, sy, sz)
        yface[slot, 0] = cube[:, 0, :]
        yface[slot, 1] = cube[:, sy - 1, :]
        turned = jnp.where(lane_half < 64, local[:, :128], local[:, sz - 128 :]).T
        zface[slot, 0] = turned[:8]
        zface[slot, 1] = turned[120:]
        if slot == 0:
            pl.semaphore_wait(barrier, greeted)
        for offset, zero, cond in around():
            guarded(cond, lambda: message(slot, offset, zero).start())
        for offset, zero, cond in around():
            guarded(cond, lambda: incoming(slot, offset, zero).wait_recv())
        value = jnp.concatenate(
            [local[:sy] + xr[slot, 0], local[sy : rows - sy], local[rows - sy :] + xr[slot, 1]],
            axis=0,
        )

        def y_side(side):
            face = yr[slot, side]
            face = face + jnp.where(x_of == 0, jnp.broadcast_to(er[slot, side][sx - 1 :], (sx, sz)), 0.0)
            face = face + jnp.where(x_of == sx - 1, jnp.broadcast_to(er[slot, 2 + side][:1], (sx, sz)), 0.0)
            return jnp.broadcast_to(face[:, None, :], (sx, sy, sz)).reshape(rows, sz)

        low = jnp.where(y_at == 0, y_side(0), pltpu.roll(value, 1, 0))
        high = jnp.where(y_at == sy - 1, y_side(1), pltpu.roll(value, rows - 1, 0))
        value = value + jnp.where(y_node == 0, low, 0.0) + jnp.where(y_node == 7, high, 0.0)
        z_low = plane(slot, 0)[7:]
        z_high = plane(slot, 1)[:1]
        ends = jnp.concatenate(
            [jnp.broadcast_to(z_low, (64, rows)), jnp.broadcast_to(z_high, (64, rows))], axis=0
        ).T
        ends = jnp.concatenate([ends] * (sz // 128), axis=1)
        low = jnp.where(lane == 0, ends, pltpu.roll(value, 1, 1))
        high = jnp.where(lane == sz - 1, ends, pltpu.roll(value, sz - 1, 1))
        return value + jnp.where(z_node == 0, low, 0.0) + jnp.where(z_node == 7, high, 0.0)

    def wait_load(*which):
        for k in which:
            loads[k].wait()

    wait_load(0, 4, 5, 6)
    scaled = coef[...] * quad[...]
    diagonal = assemble(0, from_left(sq_xy, scaled) + from_right(scaled, sq_z))
    inverse = 1.0 / diagonal
    wait_load(1, 7, 8, 9, 10)
    theta = (eig_high + eig_low) / 2.0
    delta = (eig_high - eig_low) / 2.0
    sigma = theta / delta
    residual = rhs[...]
    direction = inverse * residual * (1.0 / theta)
    smoothed = direction
    rho = 1.0 / sigma
    for sweep in range(CHEB):
        grads = from_left(f_xy, direction)
        grad_z = from_right(direction, f_z)
        flux = jnp.concatenate([scaled * grads[:rows], scaled * grads[rows:]], axis=0)
        local = from_left(b_xy, flux) + from_right(scaled * grad_z, b_z)
        residual = residual - assemble(sweep + 1, local)
        if sweep + 1 < CHEB:
            rho_new = 1.0 / (2.0 * sigma - rho)
            direction = rho_new * rho * direction + (2.0 * rho_new / delta) * inverse * residual
            smoothed = smoothed + direction
            rho = rho_new

    wait_load(2, 3)
    weight = agg[...]
    count, unknowns = factor.shape
    column = jnp.sum(weight * residual, axis=0, keepdims=True)
    member = lax.broadcasted_iota(jnp.int32, (count, sz), 1) // (sz // count)
    member = member == lax.broadcasted_iota(jnp.int32, (count, sz), 0)
    coarse_rhs = jnp.sum(jnp.where(member, column, 0.0), axis=1, keepdims=True)
    x_mat = factor[...]

    def exchanged(term, which, peers, got, send, recv):
        part[which] = term
        copies = [
            pltpu.make_async_remote_copy(
                src_ref=part.at[which],
                dst_ref=got.at[j],
                send_sem=send.at[j],
                recv_sem=recv.at[j],
                device_id=peer,
                device_id_type=MESH,
            )
            for j, peer in enumerate(peers)
        ]
        for copy in copies:
            copy.start()
        for j, copy in enumerate(copies):
            copy.wait_recv()
            term = term + got[j]
        return term, copies

    term = jnp.sum(coarse_rhs * x_mat, axis=0, keepdims=True)
    term, copies1 = exchanged(term, 0, peers1, got1, send1, recv1)
    term, copies2 = exchanged(term, 1, peers2, got2, send2, recv2)
    answer = jnp.sum(x_mat * term, axis=1, keepdims=True)
    spread = jnp.sum(jnp.where(member, answer, 0.0), axis=0, keepdims=True)
    out[...] = smoothed + weight * spread
    on_lane = lax.broadcasted_iota(jnp.int32, (count, 128), 1)
    on_lane = on_lane == lax.broadcasted_iota(jnp.int32, (count, 128), 0)
    out_c[...] = jnp.sum(jnp.where(on_lane, answer, 0.0), axis=0, keepdims=True)

    for slot in range(CHEB + 1):
        for offset, zero, cond in around():
            guarded(cond, lambda: message(slot, offset, zero).wait_send())
    for copy in copies1 + copies2:
        copy.wait_send()


def per_device(dims, right_side, coefficient, agg_weight, coarse_factor):
    sizes = right_side.shape
    sx, sy, sz = sizes
    rows = sx * sy
    gx, gy, gz = dims
    flat = [a.reshape(rows, sz) for a in (coefficient, right_side, agg_weight)]
    operands = flat + [coarse_factor] + [jnp.asarray(t) for t in tables(sx, sy, sz)]
    count, unknowns = coarse_factor.shape
    slots = CHEB + 1
    f32 = jnp.float32
    dma = pltpu.SemaphoreType.DMA
    n1, n2 = max(gx * gy - 1, 1), max(gz - 1, 1)
    update, answer = pl.pallas_call(
        functools.partial(kernel, dims, sizes),
        out_shape=[
            jax.ShapeDtypeStruct((rows, sz), f32),
            jax.ShapeDtypeStruct((1, 128), f32),
        ],
        in_specs=[pl.BlockSpec(memory_space=pl.ANY)] * len(operands),
        out_specs=[pl.BlockSpec(memory_space=pltpu.VMEM)] * 2,
        scratch_shapes=[pltpu.VMEM(o.shape, o.dtype) for o in operands]
        + [
            pltpu.VMEM((slots, rows, sz), f32),
            pltpu.VMEM((slots, 2, sx, sz), f32),
            pltpu.VMEM((slots, 2, 8, rows), f32),
            pltpu.VMEM((slots, 2, sy, sz), f32),
            pltpu.VMEM((slots, 2, sx, sz), f32),
            pltpu.VMEM((slots, 4, sx, sz), f32),
            pltpu.VMEM((slots, 2, 9, 8, rows), f32),
            pltpu.VMEM((2, 1, unknowns), f32),
            pltpu.VMEM((n1, 1, unknowns), f32),
            pltpu.VMEM((n2, 1, unknowns), f32),
            dma((len(operands),)),
            dma((slots, 27)),
            dma((slots, 27)),
            dma((n1,)),
            dma((n1,)),
            dma((n2,)),
            dma((n2,)),
        ],
        compiler_params=pltpu.CompilerParams(
            collective_id=0, has_side_effects=True, vmem_limit_bytes=48 * 1024 * 1024
        ),
        cost_estimate=pl.CostEstimate(
            flops=400_000_000, bytes_accessed=2_000_000, transcendentals=0
        ),
    )(*operands)
    return update.reshape(sizes), answer[0, :count]


def solution(mesh):
    dims = tuple(mesh.shape[a] for a in ("gx", "gy", "gz"))
    return jax.shard_map(
        functools.partial(per_device, dims),
        mesh=mesh,
        in_specs=(
            P("gx", "gy", "gz"),
            P("gx", "gy", "gz"),
            P("gx", "gy", "gz"),
            P(("gx", "gy", "gz"), None),
        ),
        out_specs=(P("gx", "gy", "gz"), P(("gx", "gy", "gz"))),
        check_vma=False,
    )
```

time: 184 us -> 49.7 us (0.27)
  waiting for transfers between devices: 70.4 us -> 0 us
  starting transfers between devices: 52.9 us -> 0 us
  blocking collectives: 37.8 us -> 0 us
  Pallas kernels: 0 us -> 37.6 us
  matrix products: 8.03 us -> 0 us
  other arithmetic: 5.7 us -> 0 us
  local copies, waits for them, and re-layouts: 6.47 us -> 11 us
    ppermute x30 -> x0, waiting for transfers between devices: 70.4 us -> none  [the longest x15 63 us: padded_2(): lax.ppermute(head, axis, [((i + 1) % count, i) for i in range(ends)])]
    ppermute x30 -> x0, starting transfers between devices: 52.9 us -> none  [the longest x15 33.5 us: padded_2(): lax.ppermute(tail, axis, [(i, (i + 1) % count) for i in range(ends)])]
    psum x1 -> x0, blocking collectives: 37.8 us -> none  [per_device(): projected = lax.psum(partial_term, ('gx', 'gy', 'gz'))]
    pallas_call x0 -> x1, Pallas kernels: none -> 37.6 us  [per_device(): pl.pallas_call(functools.partial(kernel, dims, sizes), out_shape=[jax.Sha...]
    dot_general x29 -> x0, matrix products: 8.03 us -> none  [the longest x5 1.68 us: backward_sum(): total = jnp.einsum('ai,ajk->ijk', mat_x, part_x, precision=highest)]
    unnamed x29 -> x23, local copies, waits for them, and re-layouts: 5.65 us -> 10.5 us
    concatenate x10 -> x0, other arithmetic: 1.89 us -> none  [padded_2(): jnp.concatenate([lax.ppermute(tail, axis, [(i, (i + 1) % count) for i in...]
  transfers between devices with their start and end apart: 30 -> 0, of which waited for: 25 -> 0; matrix products, arithmetic and copies ran while one was open for 0% -> 0% of each run, Pallas kernels for 0% -> 0%
where the time goes in v1:
time: 49.7 us; the launch traced here: 49.3 us
  Pallas kernels  37.6 us (76%)
  local copies, waits for them, and re-layouts  11 us (22%)
  between operations  0.66 us (1%)
    pallas_call x1, Pallas kernels, per_device(): pl.pallas_call(functools.partial(kernel, dims, sizes), out_shape=[jax.Sha...  37.6 us
    unnamed x23, local copies, waits for them, and re-layouts  10.5 us

profile of v1, /device:TPU:0, one launch (start us, length us, event | category | flops | bytes accessed | tf_op | source)
XLA Modules:
  0.0 49.3 jit_solution(3664119318174417635)
XLA Ops:
  0.6 0.0 copy-start
  0.6 0.9 %copy-done = bf16[2,256,256]{2,1,0:T(8,128)(2,1)S(1)} copy-done((bf16[2,256,256]{2,1,0:T(8,128)(2,1)S(1)}, bf16[2,256,256]{2,1,0:T(8,128)(2,1)}, u32[]{:S(2)}) %copy-start) | copy-done | bytes 262168
  1.6 0.0 copy-start.1
  1.6 0.9 %copy-done.1 = bf16[2,256,256]{2,1,0:T(8,128)(2,1)S(1)} copy-done((bf16[2,256,256]{2,1,0:T(8,128)(2,1)S(1)}, bf16[2,256,256]{2,1,0:T(8,128)(2,1)}, u32[]{:S(2)}) %copy-start.1) | copy-done | bytes 262168
  2.5 0.0 copy-start.2
  2.5 0.9 %copy-done.2 = bf16[2,256,256]{2,1,0:T(8,128)(2,1)S(1)} copy-done((bf16[2,256,256]{2,1,0:T(8,128)(2,1)S(1)}, bf16[2,256,256]{2,1,0:T(8,128)(2,1)}, u32[]{:S(2)}) %copy-start.2) | copy-done | bytes 262168
  3.5 0.0 copy-start.3
  3.5 0.9 %copy-done.3 = f32[8,16,256]{2,1,0:T(8,128)S(1)} copy-done((f32[8,16,256]{2,1,0:T(8,128)S(1)}, f32[8,16,256]{2,1,0:T(8,128)}, u32[]{:S(2)}) %copy-start.3) | copy-done | bytes 131096
  4.4 0.0 copy-start.4
  4.4 0.9 %copy-done.4 = f32[8,16,256]{2,1,0:T(8,128)S(1)} copy-done((f32[8,16,256]{2,1,0:T(8,128)S(1)}, f32[8,16,256]{2,1,0:T(8,128)}, u32[]{:S(2)}) %copy-start.4) | copy-done | bytes 131096
  5.3 0.0 copy-start.5
  5.3 0.9 %copy-done.5 = f32[8,16,256]{2,1,0:T(8,128)S(1)} copy-done((f32[8,16,256]{2,1,0:T(8,128)S(1)}, f32[8,16,256]{2,1,0:T(8,128)}, u32[]{:S(2)}) %copy-start.5) | copy-done | bytes 131096
  6.2 0.0 copy-start.6
  6.2 0.9 %copy-done.6 = bf16[2,128,256]{2,1,0:T(8,128)(2,1)S(1)} copy-done((bf16[2,128,256]{2,1,0:T(8,128)(2,1)S(1)}, bf16[2,128,256]{2,1,0:T(8,128)(2,1)}, u32[]{:S(2)}) %copy-start.6) | copy-done | bytes 131096
  7.1 0.0 copy-start.7
  7.1 0.9 %copy-done.7 = bf16[2,256,128]{2,1,0:T(8,128)(2,1)S(1)} copy-done((bf16[2,256,128]{2,1,0:T(8,128)(2,1)S(1)}, bf16[2,256,128]{2,1,0:T(8,128)(2,1)}, u32[]{:S(2)}) %copy-start.7) | copy-done | bytes 131096
  8.0 0.0 copy-start.8
  8.0 0.9 %copy-done.8 = f32[128,256]{1,0:T(8,128)S(1)} copy-done((f32[128,256]{1,0:T(8,128)S(1)}, f32[128,256]{1,0:T(8,128)}, u32[]{:S(2)}) %copy-start.8) | copy-done | bytes 131096
  8.9 0.0 copy-start.9
  8.9 0.8 %copy-done.9 = bf16[2,128,128]{2,1,0:T(8,128)(2,1)S(1)} copy-done((bf16[2,128,128]{2,1,0:T(8,128)(2,1)S(1)}, bf16[2,128,128]{2,1,0:T(8,128)(2,1)}, u32[]{:S(2)}) %copy-start.9) | copy-done | bytes 65560
  9.8 0.0 copy-start.10
  9.8 0.7 %copy-done.10 = f32[8,256]{1,0:T(8,128)S(1)} copy-done((f32[8,256]{1,0:T(8,128)S(1)}, f32[8,256]{1,0:T(8,128)}, u32[]{:S(2)}) %copy-start.10) | copy-done | bytes 8216
  10.5 37.6 %shard_map.122 = (f32[128,256]{1,0:T(8,128)S(1)}, f32[1,128]{1,0:T(1,128)S(1)}) custom-call(f32[128,256]{1,0:T(8,128)S(1)} %bitcast.6, f32[128,256]{1,0:T(8,128)S(1)} %bitcast.7, f32[128,256]{1,0:T(8,128)S(1)} %bitcast.8, f32[8,256]{1,0:T(8,128)S(1)} %copy-done.10, f32[128,256]{1,0:T(8,128)S(1)} %copy-done.8, bf16[2,128,128]{2,1,0:T(8,128)(2,1)S(1)} %copy-done.9, ...), custom_call_target="tpu_custom_call" | custom-call | flops 400000000 | bytes 2000000 | tf_op jit(solution)/shard_map/pallas_call | solution.py:370
  48.1 0.5 %slice_bitcast_fusion = f32[8]{0:T(128)} fusion(f32[1,128]{1,0:T(1,128)S(1)} %get-tuple-element.5), kind=kLoop, calls=%fused_computation | loop fusion | bytes 64 | tf_op jit(solution)/shard_map/squeeze | solution.py:405
  48.6 0.7 %copy.14 = f32[8,16,256]{2,1,0:T(8,128)} copy(f32[8,16,256]{2,1,0:T(8,128)S(1)} %bitcast.9) | data formatting | bytes 262144
Async XLA Ops:
  0.6 1.0 %copy-start = (bf16[2,256,256]{2,1,0:T(8,128)(2,1)S(1)}, bf16[2,256,256]{2,1,0:T(8,128)(2,1)}, u32[]{:S(2)}) copy-start(bf16[2,256,256]{2,1,0:T(8,128)(2,1)} %constant.20.clone.refs_10_) | copy-start | bytes 786436
  1.6 0.9 %copy-start.1 = (bf16[2,256,256]{2,1,0:T(8,128)(2,1)S(1)}, bf16[2,256,256]{2,1,0:T(8,128)(2,1)}, u32[]{:S(2)}) copy-start(bf16[2,256,256]{2,1,0:T(8,128)(2,1)} %constant.18.clone.refs_8_) | copy-start | bytes 786436
  2.5 0.9 %copy-start.2 = (bf16[2,256,256]{2,1,0:T(8,128)(2,1)S(1)}, bf16[2,256,256]{2,1,0:T(8,128)(2,1)}, u32[]{:S(2)}) copy-start(bf16[2,256,256]{2,1,0:T(8,128)(2,1)} %constant.16.clone.refs_6_) | copy-start | bytes 786436
  3.5 0.9 %copy-start.3 = (f32[8,16,256]{2,1,0:T(8,128)S(1)}, f32[8,16,256]{2,1,0:T(8,128)}, u32[]{:S(2)}) copy-start(f32[8,16,256]{2,1,0:T(8,128)} %param.12) | copy-start | bytes 393220
  4.4 0.9 %copy-start.4 = (f32[8,16,256]{2,1,0:T(8,128)S(1)}, f32[8,16,256]{2,1,0:T(8,128)}, u32[]{:S(2)}) copy-start(f32[8,16,256]{2,1,0:T(8,128)} %param.11) | copy-start | bytes 393220
  5.3 0.9 %copy-start.5 = (f32[8,16,256]{2,1,0:T(8,128)S(1)}, f32[8,16,256]{2,1,0:T(8,128)}, u32[]{:S(2)}) copy-start(f32[8,16,256]{2,1,0:T(8,128)} %param.13) | copy-start | bytes 393220
  6.2 0.9 %copy-start.6 = (bf16[2,128,256]{2,1,0:T(8,128)(2,1)S(1)}, bf16[2,128,256]{2,1,0:T(8,128)(2,1)}, u32[]{:S(2)}) copy-start(bf16[2,128,256]{2,1,0:T(8,128)(2,1)} %constant.19.clone.refs_9_) | copy-start | bytes 393220
  7.1 0.9 %copy-start.7 = (bf16[2,256,128]{2,1,0:T(8,128)(2,1)S(1)}, bf16[2,256,128]{2,1,0:T(8,128)(2,1)}, u32[]{:S(2)}) copy-start(bf16[2,256,128]{2,1,0:T(8,128)(2,1)} %constant.17.clone.refs_7_) | copy-start | bytes 393220
  8.0 0.9 %copy-start.8 = (f32[128,256]{1,0:T(8,128)S(1)}, f32[128,256]{1,0:T(8,128)}, u32[]{:S(2)}) copy-start(f32[128,256]{1,0:T(8,128)} %constant.14.clone.refs_4_) | copy-start | bytes 393220
  8.9 0.8 %copy-start.9 = (bf16[2,128,128]{2,1,0:T(8,128)(2,1)S(1)}, bf16[2,128,128]{2,1,0:T(8,128)(2,1)}, u32[]{:S(2)}) copy-start(bf16[2,128,128]{2,1,0:T(8,128)(2,1)} %constant.15.clone.refs_5_) | copy-start | bytes 196612
  9.8 0.7 %copy-start.10 = (f32[8,256]{1,0:T(8,128)S(1)}, f32[8,256]{1,0:T(8,128)}, u32[]{:S(2)}) copy-start(f32[8,256]{1,0:T(8,128)} %refs_3_.1) | copy-start | bytes 24580

commit v2 on v1

--- a/solution.py
+++ b/solution.py
@@ -13,6 +13,7 @@
 ORDER = 7
 CHEB = 4
 MESH = pl.DeviceIdType.MESH
+ONE_ROUND = 64
 eig_high = 4.0
 eig_low = 0.2
 gll_inner = np.array(
@@ -139,9 +140,12 @@
         return [(0, None), (1, index < count - 1), (-1, index > 0)]
 
     def around():
-        for (dx, cx), (dy, cy), (dz, cz) in itertools.product(
-            options(ix, gx), options(iy, gy), options(iz, gz)
-        ):
+        every = itertools.product(options(ix, gx), options(iy, gy), options(iz, gz))
+
+        def near(one):
+            return sum(isinstance(d, int) and d == 0 for d, _ in one)
+
+        for (dx, cx), (dy, cy), (dz, cz) in sorted(every, key=near):
             zero = [isinstance(d, int) and d == 0 for d in (dx, dy, dz)]
             if all(zero):
                 continue
@@ -159,14 +163,21 @@
 
     nxy = gx * gy
     me_xy = ix * gy + iy
+    one_round = nxy * gz <= ONE_ROUND
     peers1 = []
-    for j in range(1, nxy):
-        other = lax.rem(me_xy + j, nxy)
-        peers1.append((other // gy, lax.rem(other, gy), iz))
-    peers2 = [(ix, iy, lax.rem(iz + j, gz)) for j in range(1, gz)]
+    if one_round:
+        for j in range(1, nxy * gz):
+            other = lax.rem(me_xy * gz + iz + j, nxy * gz)
+            peers1.append((other // (gy * gz), lax.rem(other // gz, gy), lax.rem(other, gz)))
+        peers2 = []
+    else:
+        for j in range(1, nxy):
+            other = lax.rem(me_xy + j, nxy)
+            peers1.append((other // gy, lax.rem(other, gy), iz))
+        peers2 = [(ix, iy, lax.rem(iz + j, gz)) for j in range(1, gz)]
 
     barrier = pltpu.get_barrier_semaphore()
-    for offset, _, cond in around():
+    for offset, _, cond in [] if one_round else around():
         def greet(offset=offset):
             pl.semaphore_signal(
                 barrier,
@@ -184,7 +195,9 @@
             return count
         return 3 - (index == 0).astype(jnp.int32) - (index == count - 1).astype(jnp.int32)
 
-    greeted = present(ix, gx) * present(iy, gy) * present(iz, gz) - 1 + len(peers1) + len(peers2)
+    greeted = len(peers1) + len(peers2)
+    if not one_round:
+        greeted = greeted + present(ix, gx) * present(iy, gy) * present(iz, gz) - 1
 
     def message(slot, offset, zero):
         dx, dy, dz = offset
@@ -346,7 +359,7 @@
     out[...] = smoothed + weight * spread
     on_lane = lax.broadcasted_iota(jnp.int32, (count, 128), 1)
     on_lane = on_lane == lax.broadcasted_iota(jnp.int32, (count, 128), 0)
-    out_c[...] = jnp.sum(jnp.where(on_lane, answer, 0.0), axis=0, keepdims=True)
+    out_c[...] = jnp.sum(jnp.where(on_lane, answer, 0.0), axis=0)[:count]
 
     for slot in range(CHEB + 1):
         for offset, zero, cond in around():
@@ -367,13 +380,15 @@
     f32 = jnp.float32
     dma = pltpu.SemaphoreType.DMA
     n1, n2 = max(gx * gy - 1, 1), max(gz - 1, 1)
+    if gx * gy * gz <= ONE_ROUND:
+        n1 = max(gx * gy * gz - 1, 1)
     update, answer = pl.pallas_call(
         functools.partial(kernel, dims, sizes),
         out_shape=[
-            jax.ShapeDtypeStruct((rows, sz), f32),
-            jax.ShapeDtypeStruct((1, 128), f32),
+            pltpu.VMEM((rows, sz), f32),
+            pltpu.VMEM((count,), f32),
         ],
-        in_specs=[pl.BlockSpec(memory_space=pl.ANY)] * len(operands),
+        in_specs=[pl.BlockSpec(memory_space=pltpu.HBM)] * len(operands),
         out_specs=[pl.BlockSpec(memory_space=pltpu.VMEM)] * 2,
         scratch_shapes=[pltpu.VMEM(o.shape, o.dtype) for o in operands]
         + [
@@ -396,13 +411,13 @@
             dma((n2,)),
         ],
         compiler_params=pltpu.CompilerParams(
-            collective_id=0, has_side_effects=True, vmem_limit_bytes=48 * 1024 * 1024
+            collective_id=0, has_side_effects=True, vmem_limit_bytes=63 * 1024 * 1024
         ),
         cost_estimate=pl.CostEstimate(
             flops=400_000_000, bytes_accessed=2_000_000, transcendentals=0
         ),
     )(*operands)
-    return update.reshape(sizes), answer[0, :count]
+    return update.reshape(sizes), answer
 
 
 def solution(mesh):

time: 49.7 us -> 37.4 us (0.75)
  local copies, waits for them, and re-layouts: 11 us -> 1.17 us
  Pallas kernels: 37.6 us -> 35.4 us
    unnamed x23 -> x2, local copies, waits for them, and re-layouts: 10.5 us -> 1.17 us
    pallas_call x1, Pallas kernels: 37.6 us -> 35.4 us  [per_device(): pl.pallas_call(functools.partial(kernel, dims, sizes), out_shape=[pltpu.V...]
    squeeze x1 -> x0, local copies, waits for them, and re-layouts: 0.51 us -> none  [per_device(): return (update.reshape(sizes), answer[0, :count])]
where the time goes in v2:
time: 37.4 us; the launch traced here: 37.2 us
  Pallas kernels  35.4 us (95%)
  local copies, waits for them, and re-layouts  1.17 us (3%)
  between operations  0.64 us (2%)
    pallas_call x1, Pallas kernels, per_device(): pl.pallas_call(functools.partial(kernel, dims, sizes), out_shape=[pltpu.V...  35.4 us
    unnamed x2, local copies, waits for them, and re-layouts  1.17 us

profile of v2, /device:TPU:0, one launch (start us, length us, event | category | flops | bytes accessed | tf_op | source)
XLA Modules:
  0.0 37.2 jit_solution(16563541606978546302)
XLA Ops:
  0.6 35.4 %shard_map.122 = (f32[128,256]{1,0:T(8,128)S(1)}, f32[8]{0:T(128)S(1)}) custom-call(f32[128,256]{1,0:T(8,128)} %bitcast.5, f32[128,256]{1,0:T(8,128)} %bitcast.6, f32[128,256]{1,0:T(8,128)} %bitcast.7, f32[8,256]{1,0:T(8,128)} %refs_3_.1, f32[128,256]{1,0:T(8,128)} %constant.14.clone.refs_4_, bf16[2,128,128]{2,1,0:T(8,128)(2,1)} %constant.15.clone.refs_5_, ...), custom_call_target="tpu_custom_call" | custom-call | flops 400000000 | bytes 2000000 | tf_op jit(solution)/shard_map/pallas_call | solution.py:385
  36.0 0.7 %copy.15 = f32[8,16,256]{2,1,0:T(8,128)} copy(f32[8,16,256]{2,1,0:T(8,128)S(1)} %bitcast.4) | data formatting | bytes 262144
  36.7 0.5 %copy.16 = f32[8]{0:T(128)} copy(f32[8]{0:T(128)S(1)} %get-tuple-element.7) | data formatting | bytes 64

commit v3 on v2

--- a/solution.py
+++ b/solution.py
@@ -116,12 +116,12 @@
     sx, sy, sz = sizes
     rows = sx * sy
     inputs, (out, out_c), scratch = refs[:11], refs[11:13], refs[13:]
-    held, (field, yface, zface, xr, yr, er, zr, part, got1, got2), sems = (
+    held, (field, yface, zface, xr, yr, er, zr, xn, part, got1, got2), sems = (
         scratch[:11],
-        scratch[11:21],
-        scratch[21:],
+        scratch[11:22],
+        scratch[22:],
     )
-    in_sem, send_sem, recv_sem, send1, recv1, send2, recv2 = sems
+    in_sem, send_sem, recv_sem, sendx, recvx, send1, recv1, send2, recv2 = sems
     ix, iy, iz = (lax.axis_index(a) for a in ("gx", "gy", "gz"))
 
     loads = [pltpu.make_async_copy(i, h, in_sem.at[k]) for k, (i, h) in enumerate(zip(inputs, held))]
@@ -129,7 +129,7 @@
         load.start()
     coef, rhs, agg, factor, quad, sq_xy, sq_z, f_xy, f_z, b_xy, b_z = held
 
-    for buf in (xr, yr, er, zr):
+    for buf in (xr, yr, er, zr, xn):
         buf[...] = jnp.zeros_like(buf)
 
     def options(index, count):
@@ -227,6 +227,18 @@
     def incoming(slot, offset, zero):
         return message(slot, tuple(-d for d in offset), zero)
 
+    def rows_message(offset):
+        dx, dy, dz = offset
+        mark = (1 - dx) * 9 + (1 - dy) * 3 + (1 - dz)
+        return pltpu.make_async_remote_copy(
+            src_ref=factor,
+            dst_ref=xn.at[mark],
+            send_sem=sendx.at[mark],
+            recv_sem=recvx.at[mark],
+            device_id=(ix + dx, iy + dy, iz + dz),
+            device_id_type=MESH,
+        )
+
     row = lax.broadcasted_iota(jnp.int32, (rows, sz), 0)
     lane = lax.broadcasted_iota(jnp.int32, (rows, sz), 1)
     y_at = lax.rem(row, sy)
@@ -256,18 +268,25 @@
         node = lax.rem(p_lane, 8)
         return mine + jnp.where(node == 0, low, 0.0) + jnp.where(node == 7, high, 0.0)
 
-    def assemble(slot, local):
+    def end_rows(local):
+        return jnp.where(lane_half < 64, local[:, :128], local[:, sz - 128 :]).T
+
+    def publish(slot, local):
         field[slot] = local
         cube = local.reshape(sx, sy, sz)
         yface[slot, 0] = cube[:, 0, :]
         yface[slot, 1] = cube[:, sy - 1, :]
-        turned = jnp.where(lane_half < 64, local[:, :128], local[:, sz - 128 :]).T
+        turned = end_rows(local)
         zface[slot, 0] = turned[:8]
         zface[slot, 1] = turned[120:]
         if slot == 0:
             pl.semaphore_wait(barrier, greeted)
         for offset, zero, cond in around():
             guarded(cond, lambda: message(slot, offset, zero).start())
+
+    def assemble(slot, local, meanwhile):
+        publish(slot, local)
+        meanwhile()
         for offset, zero, cond in around():
             guarded(cond, lambda: incoming(slot, offset, zero).wait_recv())
         value = jnp.concatenate(
@@ -298,11 +317,25 @@
         for k in which:
             loads[k].wait()
 
+    def early():
+        wait_load(2, 3)
+        publish(CHEB, agg[...])
+        for offset, zero, cond in around():
+            guarded(cond, lambda: rows_message(offset).start())
+        wait_load(1, 7, 8, 9, 10)
+
+    def arrived():
+        for offset, zero, cond in around():
+            def both(offset=offset, zero=zero):
+                incoming(CHEB, offset, zero).wait_recv()
+                rows_message(tuple(-d for d in offset)).wait_recv()
+
+            guarded(cond, both)
+
     wait_load(0, 4, 5, 6)
     scaled = coef[...] * quad[...]
-    diagonal = assemble(0, from_left(sq_xy, scaled) + from_right(scaled, sq_z))
+    diagonal = assemble(0, from_left(sq_xy, scaled) + from_right(scaled, sq_z), early)
     inverse = 1.0 / diagonal
-    wait_load(1, 7, 8, 9, 10)
     theta = (eig_high + eig_low) / 2.0
     delta = (eig_high - eig_low) / 2.0
     sigma = theta / delta
@@ -315,23 +348,74 @@
         grad_z = from_right(direction, f_z)
         flux = jnp.concatenate([scaled * grads[:rows], scaled * grads[rows:]], axis=0)
         local = from_left(b_xy, flux) + from_right(scaled * grad_z, b_z)
-        residual = residual - assemble(sweep + 1, local)
         if sweep + 1 < CHEB:
+            meanwhile = arrived if sweep + 2 == CHEB else lambda: None
+            residual = residual - assemble(sweep + 1, local, meanwhile)
             rho_new = 1.0 / (2.0 * sigma - rho)
             direction = rho_new * rho * direction + (2.0 * rho_new / delta) * inverse * residual
             smoothed = smoothed + direction
             rho = rho_new
 
-    wait_load(2, 3)
     weight = agg[...]
     count, unknowns = factor.shape
-    column = jnp.sum(weight * residual, axis=0, keepdims=True)
     member = lax.broadcasted_iota(jnp.int32, (count, sz), 1) // (sz // count)
     member = member == lax.broadcasted_iota(jnp.int32, (count, sz), 0)
-    coarse_rhs = jnp.sum(jnp.where(member, column, 0.0), axis=1, keepdims=True)
+    last = CHEB
+
+    def per_aggregate(column):
+        return jnp.sum(jnp.where(member, column, 0.0), axis=1, keepdims=True)
+
+    def inner_y(value, at, axis):
+        size = value.shape[axis]
+        node = lax.rem(at, 8)
+        low = jnp.where((node == 0) & (at != 0), pltpu.roll(value, 1, axis), 0.0)
+        high = jnp.where((node == 7) & (at != sy - 1), pltpu.roll(value, size - 1, axis), 0.0)
+        return value + low + high
+
+    low = jnp.where((z_node == 0) & (lane != 0), pltpu.roll(local, 1, 1), 0.0)
+    high = jnp.where((z_node == 7) & (lane != sz - 1), pltpu.roll(local, sz - 1, 1), 0.0)
+    joined = local + low + high
+    cube = joined.reshape(sx, sy, sz)
+    y_ends = (cube[:, 0, :], cube[:, sy - 1, :])
+
+    def total(value):
+        return jnp.sum(value, axis=0, keepdims=True)
+
+    terms = [
+        (per_aggregate(total(weight * residual - inner_y(weight, y_at, 0) * joined)), factor[...])
+    ]
+    for side in range(2):
+        layer = inner_y(xr[last, side], y_at[:sy], 0)
+        own = joined[side * (rows - sy) : side * (rows - sy) + sy]
+        terms.append((-per_aggregate(total(layer * own)), xn[side * 18 + 4]))
+        terms.append((-per_aggregate(total(yr[last, side] * y_ends[side])), xn[9 + side * 6 + 1]))
+        for other in range(2):
+            line = er[last, side * 2 + other][(1 - side) * (sx - 1) : (1 - side) * (sx - 1) + 1]
+            own = y_ends[other][side * (sx - 1) : side * (sx - 1) + 1]
+            terms.append((-per_aggregate(line * own), xn[side * 18 + other * 6 + 1]))
+
+    turned = end_rows(local)
+    tile_row = lax.broadcasted_iota(jnp.int32, (8, 1), 0)
+    for side in range(2):
+        own = jnp.broadcast_to(turned[side * 127 : side * 127 + 1], (8, rows))
+        for a, b in itertools.product(range(3), range(3)):
+            face = zr[last, side, a * 3 + b]
+            if a == 0:
+                face = jnp.where(p_lane < sy, pltpu.roll(face, sy, 1), 0.0)
+            elif a == 2:
+                face = jnp.where(p_lane >= rows - sy, pltpu.roll(face, rows - sy, 1), 0.0)
+            if b == 0:
+                face = jnp.where(p_y == 0, pltpu.roll(face, rows - (sy - 1), 1), 0.0)
+            elif b == 2:
+                face = jnp.where(p_y == sy - 1, pltpu.roll(face, sy - 1, 1), 0.0)
+            else:
+                face = inner_y(face, p_y, 1)
+            amount = jnp.sum(face * own, axis=1, keepdims=True)
+            amount = jnp.where(tile_row == 7 * (1 - side), amount, 0.0)
+            terms.append((-amount, xn[a * 9 + b * 3 + side * 2]))
     x_mat = factor[...]
 
-    def exchanged(term, which, peers, got, send, recv):
+    def exchanged(term, which, peers, got, send, recv, meanwhile):
         part[which] = term
         copies = [
             pltpu.make_async_remote_copy(
@@ -346,14 +430,27 @@
         ]
         for copy in copies:
             copy.start()
+        meanwhile()
         for j, copy in enumerate(copies):
             copy.wait_recv()
             term = term + got[j]
         return term, copies
 
-    term = jnp.sum(coarse_rhs * x_mat, axis=0, keepdims=True)
-    term, copies1 = exchanged(term, 0, peers1, got1, send1, recv1)
-    term, copies2 = exchanged(term, 1, peers2, got2, send2, recv2)
+    def drain():
+        for offset, zero, cond in around():
+            def all_slots(offset=offset, zero=zero):
+                for slot in range(CHEB + 1):
+                    message(slot, offset, zero).wait_send()
+                rows_message(offset).wait_send()
+
+            guarded(cond, all_slots)
+
+    weighed = terms[0][0] * terms[0][1]
+    for amount, block in terms[1:]:
+        weighed = weighed + amount * block
+    term = jnp.sum(weighed, axis=0, keepdims=True)
+    term, copies1 = exchanged(term, 0, peers1, got1, send1, recv1, drain)
+    term, copies2 = exchanged(term, 1, peers2, got2, send2, recv2, lambda: None)
     answer = jnp.sum(x_mat * term, axis=1, keepdims=True)
     spread = jnp.sum(jnp.where(member, answer, 0.0), axis=0, keepdims=True)
     out[...] = smoothed + weight * spread
@@ -361,9 +458,6 @@
     on_lane = on_lane == lax.broadcasted_iota(jnp.int32, (count, 128), 0)
     out_c[...] = jnp.sum(jnp.where(on_lane, answer, 0.0), axis=0)[:count]
 
-    for slot in range(CHEB + 1):
-        for offset, zero, cond in around():
-            guarded(cond, lambda: message(slot, offset, zero).wait_send())
     for copy in copies1 + copies2:
         copy.wait_send()
 
@@ -399,12 +493,15 @@
             pltpu.VMEM((slots, 2, sx, sz), f32),
             pltpu.VMEM((slots, 4, sx, sz), f32),
             pltpu.VMEM((slots, 2, 9, 8, rows), f32),
+            pltpu.VMEM((27, count, unknowns), f32),
             pltpu.VMEM((2, 1, unknowns), f32),
             pltpu.VMEM((n1, 1, unknowns), f32),
             pltpu.VMEM((n2, 1, unknowns), f32),
             dma((len(operands),)),
             dma((slots, 27)),
             dma((slots, 27)),
+            dma((27,)),
+            dma((27,)),
             dma((n1,)),
             dma((n1,)),
             dma((n2,)),

time: 37.4 us -> 34.9 us (0.933)
  Pallas kernels: 35.4 us -> 32.9 us
    pallas_call x1, Pallas kernels: 35.4 us -> 32.9 us  [per_device(): pl.pallas_call(functools.partial(kernel, dims, sizes), out_shape=[pltpu.V...]
where the time goes in v3:
time: 34.9 us; the launch traced here: 34.7 us
  Pallas kernels  32.9 us (94%)
  local copies, waits for them, and re-layouts  1.17 us (3%)
  between operations  0.64 us (2%)
    pallas_call x1, Pallas kernels, per_device(): pl.pallas_call(functools.partial(kernel, dims, sizes), out_shape=[pltpu.V...  32.9 us
    unnamed x2, local copies, waits for them, and re-layouts  1.17 us

profile of v3, /device:TPU:0, one launch (start us, length us, event | category | flops | bytes accessed | tf_op | source)
XLA Modules:
  0.0 34.7 jit_solution(540316774655062819)
XLA Ops:
  0.6 32.9 %shard_map.122 = (f32[128,256]{1,0:T(8,128)S(1)}, f32[8]{0:T(128)S(1)}) custom-call(f32[128,256]{1,0:T(8,128)} %bitcast.5, f32[128,256]{1,0:T(8,128)} %bitcast.6, f32[128,256]{1,0:T(8,128)} %bitcast.7, f32[8,256]{1,0:T(8,128)} %refs_3_.1, f32[128,256]{1,0:T(8,128)} %constant.14.clone.refs_4_, bf16[2,128,128]{2,1,0:T(8,128)(2,1)} %constant.15.clone.refs_5_, ...), custom_call_target="tpu_custom_call" | custom-call | flops 400000000 | bytes 2000000 | tf_op jit(solution)/shard_map/pallas_call | solution.py:479
  33.6 0.7 %copy.15 = f32[8,16,256]{2,1,0:T(8,128)} copy(f32[8,16,256]{2,1,0:T(8,128)S(1)} %bitcast.4) | data formatting | bytes 262144
  34.2 0.5 %copy.16 = f32[8]{0:T(128)} copy(f32[8]{0:T(128)S(1)} %get-tuple-element.7) | data formatting | bytes 64

commit v4 on v3

--- a/solution.py
+++ b/solution.py
@@ -103,12 +103,16 @@
 
 def from_left(mat, value):
     high, low = split(value)
-    return dot(mat[0], high) + (dot(mat[0], low) + dot(mat[1], high))
+    size = mat.shape[1]
+    both = dot(jnp.concatenate([mat[0], mat[1]], axis=0), high)
+    return both[:size] + (both[size:] + dot(mat[0], low))
 
 
 def from_right(value, mat):
     high, low = split(value)
-    return dot(high, mat[0]) + (dot(low, mat[0]) + dot(high, mat[1]))
+    size = value.shape[0]
+    both = dot(jnp.concatenate([high, low], axis=0), mat[0])
+    return both[:size] + (both[size:] + dot(high, mat[1]))
 
 
 def kernel(dims, sizes, *refs):
@@ -125,8 +129,6 @@
     ix, iy, iz = (lax.axis_index(a) for a in ("gx", "gy", "gz"))
 
     loads = [pltpu.make_async_copy(i, h, in_sem.at[k]) for k, (i, h) in enumerate(zip(inputs, held))]
-    for load in loads:
-        load.start()
     coef, rhs, agg, factor, quad, sq_xy, sq_z, f_xy, f_z, b_xy, b_z = held
 
     for buf in (xr, yr, er, zr, xn):
@@ -189,6 +191,9 @@
         guarded(cond, greet)
     for peer in peers1 + peers2:
         pl.semaphore_signal(barrier, inc=1, device_id=peer, device_id_type=MESH)
+
+    for k in (0, 6, 4, 5, 2, 3, 1, 7, 8, 9, 10):
+        loads[k].start()
 
     def present(index, count):
         if count <= 2:
@@ -320,9 +325,11 @@
     def early():
         wait_load(2, 3)
         publish(CHEB, agg[...])
+        wait_load(1, 7, 8, 9, 10)
+
+    def spread_rows():
         for offset, zero, cond in around():
             guarded(cond, lambda: rows_message(offset).start())
-        wait_load(1, 7, 8, 9, 10)
 
     def arrived():
         for offset, zero, cond in around():
@@ -349,7 +356,7 @@
         flux = jnp.concatenate([scaled * grads[:rows], scaled * grads[rows:]], axis=0)
         local = from_left(b_xy, flux) + from_right(scaled * grad_z, b_z)
         if sweep + 1 < CHEB:
-            meanwhile = arrived if sweep + 2 == CHEB else lambda: None
+            meanwhile = arrived if sweep + 2 == CHEB else spread_rows if sweep == 0 else lambda: None
             residual = residual - assemble(sweep + 1, local, meanwhile)
             rho_new = 1.0 / (2.0 * sigma - rho)
             direction = rho_new * rho * direction + (2.0 * rho_new / delta) * inverse * residual

time: 34.9 us -> 34.6 us (level)
  no operation moved by 1% of the time
where the time goes in v4:
time: 34.6 us; the launch traced here: 34.4 us
  Pallas kernels  32.6 us (94%)
  local copies, waits for them, and re-layouts  1.17 us (3%)
  between operations  0.64 us (2%)
    pallas_call x1, Pallas kernels, per_device(): pl.pallas_call(functools.partial(kernel, dims, sizes), out_shape=[pltpu.V...  32.6 us
    unnamed x2, local copies, waits for them, and re-layouts  1.17 us

profile of v4, /device:TPU:0, one launch (start us, length us, event | category | flops | bytes accessed | tf_op | source)
XLA Modules:
  0.0 34.4 jit_solution(6542110291226889333)
XLA Ops:
  0.6 32.6 %shard_map.122 = (f32[128,256]{1,0:T(8,128)S(1)}, f32[8]{0:T(128)S(1)}) custom-call(f32[128,256]{1,0:T(8,128)} %bitcast.5, f32[128,256]{1,0:T(8,128)} %bitcast.6, f32[128,256]{1,0:T(8,128)} %bitcast.7, f32[8,256]{1,0:T(8,128)} %refs_3_.1, f32[128,256]{1,0:T(8,128)} %constant.14.clone.refs_4_, bf16[2,128,128]{2,1,0:T(8,128)(2,1)} %constant.15.clone.refs_5_, ...), custom_call_target="tpu_custom_call" | custom-call | flops 400000000 | bytes 2000000 | tf_op jit(solution)/shard_map/pallas_call | solution.py:486
  33.3 0.7 %copy.15 = f32[8,16,256]{2,1,0:T(8,128)} copy(f32[8,16,256]{2,1,0:T(8,128)S(1)} %bitcast.4) | data formatting | bytes 262144
  33.9 0.5 %copy.16 = f32[8]{0:T(128)} copy(f32[8]{0:T(128)S(1)} %get-tuple-element.7) | data formatting | bytes 64
